TPU v7x, 32 devices: a whole 2x2x4 slice. The times are simulated.
32 devices in a mesh: ra: 8 (over z, core), dec: 4 (over y, x).
Axes of the slice: x: 2, y: 2, z: 4, core: 2. Of those that a mesh axis runs over, the one named last changes fastest.
Arguments:
- template: float32 [1024, 8192], P('dec', 'ra'), may hold values from -9 to 9
- science: float32 [1024, 8192], P('dec', 'ra'), may hold values from -12 to 12
- offsets: int32 [8, 4], P('ra', 'dec'), may hold values from 0 to 512, as said below
- source_dest: int32 [1024, 1], P(('ra', 'dec')), may hold values from 0 to 31; in each aligned block of 32 rows (0 to 31, 32 to 63, ...) at most 2 rows name the same one
- source_row: int32 [1024], P(('ra', 'dec')), may hold values from 0 to 192
- source_col: int32 [1024], P(('ra', 'dec')), may hold values from 0 to 960
Outputs:
- difference: float32 [1024, 8192], P('dec', 'ra')
- stamps: bfloat16 [32, 32, 2, 4096], P(('ra', 'dec'))
Inputs may be any that keep to these rules, and one draw needn't show every extreme that they name: `offsets`: some tile has offset 512 in every draw, and at every ra index some band has offset 0. `source_dest`: the owner is a device number in the order of the sources; at most 2 sources of one tile name the same owner, and some tile sends 2 to one owner.
All inputs are finite; a program needn't handle non-finite values.
Results may differ from a plain program's by a relative error of at most 0.001.
Values may be sent and summed in bfloat16 or wider, within the bound.
A program may use at most 192 MiB of HBM per device.

v0:
```python
import functools

import jax
import jax.numpy as jnp
import ml_dtypes
import numpy as np
from jax import lax
from jax.experimental import pallas as pl
from jax.experimental.pallas import tpu as pltpu
from jax.sharding import PartitionSpec as P

MARGIN = 15
TAPS = 31
CUT = 64
CAP = 2
OFFMAX = 512
LANE = 128
EDGE = 16
RIGHT = 640
STEP = 96
DEEP = 128
GROUP = 16
COUNT = 19
MESH = pl.DeviceIdType.MESH

gauss_widths = (1.0, 2.5, 5.0)
ridge_scale = 0.02


def filter_bank():
    t = np.arange(TAPS, dtype=np.float64) - MARGIN
    rows = []
    for w in gauss_widths:
        p = np.exp(-t * t / (2.0 * w * w))
        p = p / p.sum()
        rows += [p, p * (t / w), p * (t / w) ** 2]
    return np.stack(rows)


def split16(x):
    hi = x.astype(np.float32).astype(ml_dtypes.bfloat16)
    lo = (x - hi.astype(np.float64)).astype(np.float32).astype(ml_dtypes.bfloat16)
    return hi, lo


def tables():
    f = filter_bank()
    p = np.arange(2 * LANE)[:, None]
    x = np.arange(LANE)[None, :]
    gap = p - x
    inside = (gap >= 0) & (gap < TAPS)
    picked = np.where(inside, np.clip(gap, 0, TAPS - 1), 0)
    wide = np.concatenate([np.where(inside, f[k][picked], 0.0) for k in range(9)], 1)
    hi, lo = split16(wide)
    across = np.concatenate([hi, hi, lo], 0)
    y = np.arange(STEP)[:, None]
    q = np.arange(DEEP)[None, :]
    gap = q - y - 1
    inside = (gap >= 0) & (gap < TAPS)
    picked = np.where(inside, np.clip(gap, 0, TAPS - 1), 0)
    tall = np.stack([np.where(inside, f[k][picked], 0.0) for k in range(9)], 0)
    hi, lo = split16(tall)
    return across, np.concatenate([hi, lo], 2), tall.astype(np.float32)


def halo_kernel(n_ra, n_dec, t_ref, out_ref, zero, ssem, rsem, lsem):
    r = lax.axis_index("ra")
    d = lax.axis_index("dec")
    rows, cols = t_ref.shape
    left = lax.rem(r + n_ra - 1, n_ra)
    right = lax.rem(r + 1, n_ra)
    barrier = pltpu.get_barrier_semaphore()
    has_up = d > 0
    has_down = d < n_dec - 1

    def greet(a, b):
        pl.semaphore_signal(barrier, inc=1, device_id={"ra": a, "dec": b}, device_id_type=MESH)

    greet(left, d)
    greet(right, d)

    @pl.when(has_up)
    def _():
        for a in (left, r, right):
            greet(a, d - 1)

    @pl.when(has_down)
    def _():
        for a in (left, r, right):
            greet(a, d + 1)

    zero[...] = jnp.zeros_like(zero)
    own = pltpu.make_async_copy(
        t_ref, out_ref.at[pl.ds(EDGE, rows), pl.ds(LANE, cols)], lsem.at[0]
    )
    own.start()
    blank_up = pltpu.make_async_copy(zero, out_ref.at[pl.ds(0, EDGE), :], lsem.at[1])
    blank_down = pltpu.make_async_copy(zero, out_ref.at[pl.ds(EDGE + rows, EDGE), :], lsem.at[2])

    @pl.when(jnp.logical_not(has_up))
    def _():
        blank_up.start()

    @pl.when(jnp.logical_not(has_down))
    def _():
        blank_down.start()

    peers = 2 + 3 * has_up.astype(jnp.int32) + 3 * has_down.astype(jnp.int32)
    pl.semaphore_wait(barrier, peers)

    spans = (
        (left, pl.ds(0, RIGHT), pl.ds(LANE + cols, RIGHT)),
        (r, pl.ds(0, cols), pl.ds(LANE, cols)),
        (right, pl.ds(cols - LANE, LANE), pl.ds(0, LANE)),
    )
    bands = (
        (d - 1, pl.ds(0, EDGE), pl.ds(EDGE + rows, EDGE)),
        (d, pl.ds(0, rows), pl.ds(EDGE, rows)),
        (d + 1, pl.ds(rows - EDGE, EDGE), pl.ds(0, EDGE)),
    )

    def copy(v, h):
        to_ra, c_src, c_dst = spans[h]
        to_dec, r_src, r_dst = bands[v]
        number = v * 3 + h
        return pltpu.make_async_remote_copy(
            src_ref=t_ref.at[r_src, c_src],
            dst_ref=out_ref.at[r_dst, c_dst],
            send_sem=ssem.at[number],
            recv_sem=rsem.at[number],
            device_id={"ra": to_ra, "dec": to_dec},
            device_id_type=MESH,
        )

    copy(1, 0).start()
    copy(1, 2).start()

    @pl.when(has_up)
    def _():
        for h in range(3):
            copy(0, h).start()

    @pl.when(has_down)
    def _():
        for h in range(3):
            copy(2, h).start()

    @pl.when(has_up)
    def _():
        for h in range(3):
            copy(0, h).wait_send()
            copy(2, h).wait_recv()

    @pl.when(has_down)
    def _():
        for h in range(3):
            copy(2, h).wait_send()
            copy(0, h).wait_recv()

    @pl.when(jnp.logical_not(has_up))
    def _():
        blank_up.wait()

    @pl.when(jnp.logical_not(has_down))
    def _():
        blank_down.wait()

    own.wait()
    copy(1, 2).wait()
    copy(1, 0).wait()


def halo(template, n_ra, n_dec):
    rows, cols = template.shape
    shape = (rows + 2 * EDGE, LANE + cols + RIGHT)
    return pl.pallas_call(
        functools.partial(halo_kernel, n_ra, n_dec),
        out_shape=jax.ShapeDtypeStruct(shape, jnp.float32),
        in_specs=[pl.BlockSpec(memory_space=pl.ANY)],
        out_specs=pl.BlockSpec(memory_space=pl.ANY),
        scratch_shapes=[
            pltpu.VMEM((EDGE, shape[1]), jnp.float32),
            pltpu.SemaphoreType.DMA((9,)),
            pltpu.SemaphoreType.DMA((9,)),
            pltpu.SemaphoreType.DMA((3,)),
        ],
        compiler_params=pltpu.CompilerParams(collective_id=0, has_side_effects=True),
        name="halo",
    )(template)


def tile_kernel(
    off_ref, dest_ref, row_ref, col_ref, joined, science, across, down2, down,
    diff_ref, out_ref,
    window, r_hi, r_lo, images, gram, padded, mix, tally,
):
    rows, cols = science.shape
    tall = rows + 2 * EDGE
    deep = r_hi.shape[1]
    sources = row_ref.shape[0]
    owners = out_ref.shape[0] // CAP
    blocks = cols // LANE
    f32, bf16 = jnp.float32, jnp.bfloat16

    start = LANE - MARGIN + off_ref[0, 0]
    base = start // LANE
    shift = start % LANE
    lane = lax.broadcasted_iota(jnp.int32, (tall, LANE), 1)

    def turned(c):
        at = pl.multiple_of((base + c) * LANE, LANE)
        return pltpu.roll(joined[:, pl.ds(at, LANE)], lax.rem(LANE - shift, LANE), 1)

    before = turned(0)
    for c in range(blocks + 1):
        after = turned(c + 1)
        value = jnp.where(lane < LANE - shift, before, after)
        hi = value.astype(bf16)
        window[0, :, c * LANE : (c + 1) * LANE] = hi
        window[1, :, c * LANE : (c + 1) * LANE] = (value - hi.astype(f32)).astype(bf16)
        before = after

    r_hi[:, tall:, :] = jnp.zeros((9, deep - tall, cols), bf16)
    r_lo[:, tall:, :] = jnp.zeros((9, deep - tall, cols), bf16)

    @pl.loop(0, blocks)
    def _(b):
        at = pl.multiple_of(b * LANE, LANE)
        hi = window[0, :, pl.ds(at, 2 * LANE)]
        lo = window[1, :, pl.ds(at, 2 * LANE)]
        left = jnp.concatenate([hi, lo, hi], 1)
        for g in range(3):
            product = jnp.dot(
                left, across[:, 3 * g * LANE : 3 * (g + 1) * LANE], preferred_element_type=f32
            )
            for i in range(3):
                part = product[:, i * LANE : (i + 1) * LANE]
                top = part.astype(bf16)
                r_hi[3 * g + i, 0:tall, pl.ds(at, LANE)] = top
                r_lo[3 * g + i, 0:tall, pl.ds(at, LANE)] = (part - top.astype(f32)).astype(bf16)

    gram[...] = jnp.zeros_like(gram)
    images[18] = jnp.ones((STEP, cols), bf16)
    chunk = min(cols, 2 * LANE)
    for y0 in range(0, rows, STEP):
        size = min(STEP, rows - y0)
        images[19, 0:size, :] = science[y0 : y0 + size, :].astype(bf16)

        @pl.loop(0, cols // chunk)
        def _(n):
            at = pl.multiple_of(n * chunk, chunk)
            k = 0
            for g in range(3):
                for i in range(3):
                    part = r_hi[3 * g + i, y0 : y0 + DEEP, pl.ds(at, chunk)]
                    count = 3 - i
                    left = down2[3 * g : 3 * g + count].reshape(count * STEP, 2 * DEEP)
                    product = jnp.dot(
                        left, jnp.concatenate([part, part], 0), preferred_element_type=f32
                    )
                    images[k : k + count, :, pl.ds(at, chunk)] = product.astype(bf16).reshape(
                        count, STEP, chunk
                    )
                    k = k + count

        @pl.loop(0, size // GROUP)
        def _(q):
            at = pl.multiple_of(q * GROUP, GROUP)
            stack = images[:, pl.ds(at, GROUP), :].reshape(20 * GROUP, cols)
            gram[...] += lax.dot_general(
                stack, stack, (((1,), (1,)), ((), ())), preferred_element_type=f32
            )

    length = 20 * GROUP
    ri = lax.broadcasted_iota(jnp.int32, (length, length), 0)
    ci = lax.broadcasted_iota(jnp.int32, (length, length), 1)
    kept = jnp.where(ri % GROUP == ci % GROUP, gram[...], 0.0)
    kept = jnp.sum(kept.reshape(20, GROUP, length), axis=1)
    pick = (
        lax.broadcasted_iota(jnp.int32, (length, LANE), 0) // GROUP
        == lax.broadcasted_iota(jnp.int32, (length, LANE), 1)
    ).astype(f32)
    system = jnp.dot(kept, pick, precision=lax.Precision.HIGHEST, preferred_element_type=f32)

    rr = lax.broadcasted_iota(jnp.int32, (20, LANE), 0)
    cc = lax.broadcasted_iota(jnp.int32, (20, LANE), 1)
    diagonal = (rr == cc) & (rr < COUNT)
    trace = jnp.sum(jnp.where(diagonal, system, 0.0), axis=(0, 1), keepdims=True)
    system = system + jnp.where(diagonal, ridge_scale * trace / COUNT, 0.0)
    for k in range(COUNT):
        pivot = system[k : k + 1, :] / system[k : k + 1, k : k + 1]
        system = jnp.where(rr == k, pivot, system - system[:, k : k + 1] * pivot)

    def weight(k):
        return system[k : k + 1, 19:20]

    k = 0
    for g in range(3):
        for i in range(3):
            total = jnp.zeros((STEP, DEEP), f32)
            for j in range(3 - i):
                total = total + weight(k) * down[3 * g + j]
                k = k + 1
            hi = total.astype(bf16)
            at = (3 * g + i) * DEEP
            mix[0:STEP, at : at + DEEP] = hi
            mix[STEP : 2 * STEP, at : at + DEEP] = (total - hi.astype(f32)).astype(bf16)
    flat = weight(18)

    for y0 in range(0, rows, STEP):
        size = min(STEP, rows - y0)

        for n in range(cols // chunk):
            at = n * chunk
            right = r_hi[:, y0 : y0 + DEEP, at : at + chunk].reshape(9 * DEEP, chunk)
            rest = r_lo[:, y0 : y0 + DEEP, at : at + chunk].reshape(9 * DEEP, chunk)
            both = jnp.dot(mix[...], right, preferred_element_type=f32)
            model = (
                both[0:STEP]
                + both[STEP:]
                + jnp.dot(mix[0:STEP, :], rest, preferred_element_type=f32)
            )
            value = science[y0 : y0 + size, at : at + chunk] - (model[0:size] + flat)
            diff_ref[y0 : y0 + size, at : at + chunk] = value
            for c in range(chunk // LANE):
                padded[at // LANE + c, y0 : y0 + size, :] = value[:, c * LANE : (c + 1) * LANE]

    out_ref[...] = jnp.zeros_like(out_ref)

    @pl.loop(0, owners)
    def _(e):
        tally[e] = 0

    lane2 = lax.broadcasted_iota(jnp.int32, (CUT // 2, LANE), 1)

    @pl.loop(0, sources)
    def _(n):
        owner = dest_ref[n, 0]
        slot = tally[owner]
        tally[owner] = slot + 1
        row = row_ref[n]
        col = col_ref[n]
        tile = col // LANE
        s = col % LANE
        first = lax.rem(LANE - s, LANE)
        second = lax.rem(LANE + CUT - s, LANE)

        def half(r0, turn, bound):
            a = pltpu.roll(padded[tile, pl.ds(r0, CUT // 2, stride=2), :], turn, 1)
            b = pltpu.roll(padded[tile + 1, pl.ds(r0, CUT // 2, stride=2), :], turn, 1)
            return jnp.where(lane2 < bound, a, b)

        even = half(row, first, LANE - s)
        odd = half(row + 1, second, LANE + CUT - s)
        stamp = jnp.where(lane2 < CUT, even, odd)
        out_ref[owner * CAP + slot] = stamp.astype(bf16)


def tile(joined, science, offsets, dest, row, col, devices):
    rows, cols = science.shape
    across, down2, down = tables()
    smem = pl.BlockSpec(memory_space=pltpu.SMEM)
    vmem = pl.BlockSpec(memory_space=pltpu.VMEM)
    deep = -(-rows // STEP) * STEP + DEEP - STEP
    bf16 = jnp.bfloat16
    return pl.pallas_call(
        tile_kernel,
        out_shape=(
            jax.ShapeDtypeStruct((rows, cols), jnp.float32),
            jax.ShapeDtypeStruct((devices * CAP, CUT // 2, LANE), bf16),
        ),
        in_specs=[smem] * 4 + [vmem] * 5,
        out_specs=(vmem, vmem),
        scratch_shapes=[
            pltpu.VMEM((2, rows + 2 * EDGE, cols + LANE), bf16),
            pltpu.VMEM((9, deep, cols), bf16),
            pltpu.VMEM((9, deep, cols), bf16),
            pltpu.VMEM((20, STEP, cols), bf16),
            pltpu.VMEM((20 * GROUP, 20 * GROUP), jnp.float32),
            pltpu.VMEM((cols // LANE + 1, rows, LANE), jnp.float32),
            pltpu.VMEM((2 * STEP, 9 * DEEP), bf16),
            pltpu.SMEM((devices,), jnp.int32),
        ],
        compiler_params=pltpu.CompilerParams(vmem_limit_bytes=52 * 1024 * 1024),
        name="tile",
    )(offsets, dest, row, col, joined, science, jnp.asarray(across), jnp.asarray(down2), jnp.asarray(down))


def exchange_kernel(n_ra, n_dec, in_ref, out_ref, ssem, rsem, lsem):
    me = lax.axis_index("ra") * n_dec + lax.axis_index("dec")
    devices = n_ra * n_dec
    barrier = pltpu.get_barrier_semaphore()

    def place(t):
        return {"ra": t // n_dec, "dec": t % n_dec}

    @pl.loop(1, devices)
    def _(k):
        pl.semaphore_signal(
            barrier, inc=1, device_id=place(lax.rem(me + k, devices)), device_id_type=MESH
        )

    own = pltpu.make_async_copy(in_ref.at[me], out_ref.at[me], lsem.at[0])
    own.start()
    pl.semaphore_wait(barrier, devices - 1)

    def copy(k, block):
        target = lax.rem(me + k, devices)
        return pltpu.make_async_remote_copy(
            src_ref=in_ref.at[target],
            dst_ref=out_ref.at[block],
            send_sem=ssem.at[k],
            recv_sem=rsem.at[k],
            device_id=place(target),
            device_id_type=MESH,
        )

    @pl.loop(1, devices)
    def _(k):
        copy(k, me).start()

    @pl.loop(1, devices)
    def _(k):
        copy(k, me).wait_send()
        copy(k, lax.rem(me + devices - k, devices)).wait_recv()

    own.wait()


def exchange(outgoing, n_ra, n_dec):
    devices = n_ra * n_dec
    return pl.pallas_call(
        functools.partial(exchange_kernel, n_ra, n_dec),
        out_shape=jax.ShapeDtypeStruct(outgoing.shape, outgoing.dtype),
        in_specs=[pl.BlockSpec(memory_space=pl.ANY)],
        out_specs=pl.BlockSpec(memory_space=pl.ANY),
        scratch_shapes=[
            pltpu.SemaphoreType.DMA((devices,)),
            pltpu.SemaphoreType.DMA((devices,)),
            pltpu.SemaphoreType.DMA((1,)),
        ],
        compiler_params=pltpu.CompilerParams(collective_id=1, has_side_effects=True),
        name="exchange",
    )(outgoing)


def solution(mesh):
    n_ra, n_dec = mesh.shape["ra"], mesh.shape["dec"]
    devices = n_ra * n_dec

    def per_device(template, science, offsets, source_dest, source_row, source_col):
        joined = halo(template, n_ra, n_dec)
        difference, outgoing = tile(
            joined, science, offsets, source_dest, source_row, source_col, devices
        )
        received = exchange(outgoing.reshape(devices, CAP, CUT // 2, LANE), n_ra, n_dec)
        return difference, received.reshape(1, devices, CAP, CUT * CUT)

    placed = (
        P("dec", "ra"),
        P("dec", "ra"),
        P("ra", "dec"),
        P(("ra", "dec"), None),
        P(("ra", "dec")),
        P(("ra", "dec")),
    )
    return jax.shard_map(
        per_device,
        mesh=mesh,
        in_specs=placed,
        out_specs=(P("dec", "ra"), P(("ra", "dec"), None, None, None)),
        check_vma=False,
    )
```

profile of v0, /device:TPU:15, one launch (start us, length us, event | category | flops | bytes accessed | tf_op | source)
XLA Modules:
  0.0 89.4 jit_solution(6194669882722943291)
XLA Ops:
  0.6 0.0 copy-start.1
  0.6 0.0 copy-start.2
  0.7 0.0 copy-start.4
  0.7 0.0 copy-start.3
  1.4 0.7 copy.11.dest_ref
  2.1 33.1 %halo.1.joined = f32[288,1792]{1,0:T(8,128)} custom-call(f32[256,1024]{1,0:T(8,128)} %t_ref.1), custom_call_target="tpu_custom_call" | custom-call | tf_op jit(solution)/shard_map/halo/pallas_call | solution.py:176
  35.2 0.0 copy-done.1
  35.2 0.0 copy-done.2
  35.2 0.0 copy-done.4
  35.2 0.0 copy-done.3
  35.2 33.3 %tile.1 = (f32[256,1024]{1,0:T(8,128)}, bf16[64,32,128]{2,1,0:T(8,128)(2,1)S(1)}) custom-call(s32[1,1]{1,0:T(1,128)S(6)} %copy.12.off_ref, s32[32,1]{1,0:T(8,128)S(1)} %copy.11.dest_ref, s32[32]{0:T(128)S(1)} %copy-done.3, s32[32]{0:T(128)S(1)} %copy-done.4, f32[288,1792]{1,0:T(8,128)} %halo.1.joined, f32[256,1024]{1,0:T(8,128)} %science.1, ...), custom_call_target="tpu_custom_call" | custom-call | tf_op jit(solution)/shard_map/tile/pallas_call | solution.py:366
  68.6 0.0 copy-start
  68.6 0.8 copy-done
  69.4 18.1 %exchange.1 = bf16[32,2,32,128]{3,2,1,0:T(8,128)(2,1)} custom-call(bf16[32,2,32,128]{3,2,1,0:T(8,128)(2,1)} %bitcast.3), custom_call_target="tpu_custom_call" | custom-call | tf_op jit(solution)/shard_map/exchange/pallas_call | solution.py:432
  87.4 2.0 %reshape.11 = bf16[1,32,2,4096]{3,2,1,0:T(2,128)(2,1)} reshape(bf16[32,2,32,128]{3,2,1,0:T(8,128)(2,1)} %exchange.1) | data formatting | bytes 1048576 | tf_op jit(solution)/shard_map/reshape | solution.py:457
Async XLA Ops:
  0.6 34.6 %copy-start.1 = (f32[9,96,128]{2,1,0:T(8,128)S(1)}, f32[9,96,128]{2,1,0:T(8,128)}, u32[]{:S(2)}) copy-start(f32[9,96,128]{2,1,0:T(8,128)} %constant.8.clone.down) | copy-start | bytes 1327108
  0.6 34.6 %copy-start.2 = (bf16[9,96,256]{2,1,0:T(8,128)(2,1)S(1)}, bf16[9,96,256]{2,1,0:T(8,128)(2,1)}, u32[]{:S(2)}) copy-start(bf16[9,96,256]{2,1,0:T(8,128)(2,1)} %constant.7.clone.down2) | copy-start | bytes 1327108
  0.7 34.6 %copy-start.4 = (s32[32]{0:T(128)S(1)}, s32[32]{0:T(128)}, u32[]{:S(2)}) copy-start(s32[32]{0:T(128)} %col_ref.1) | copy-start | bytes 388
  0.7 34.6 %copy-start.3 = (s32[32]{0:T(128)S(1)}, s32[32]{0:T(128)}, u32[]{:S(2)}) copy-start(s32[32]{0:T(128)} %row_ref.1) | copy-start | bytes 388
  68.6 0.8 copy-start
where the time goes:
time: 89.6 us; the launch traced here: 89.4 us
  Pallas kernels  84.5 us (94%)
  local copies, waits for them, and re-layouts  3.51 us (4%)
  between operations  1.43 us (2%)
    pallas_call x1, Pallas kernels, tile(): pl.pallas_call(tile_kernel, out_shape=(jax.ShapeDtypeStruct((rows, cols),...  33.3 us
    pallas_call x1, Pallas kernels, halo(): pl.pallas_call(functools.partial(halo_kernel, n_ra, n_dec), out_shape=jax...  33.1 us
    pallas_call x1, Pallas kernels, exchange(): pl.pallas_call(functools.partial(exchange_kernel, n_ra, n_dec), out_shape...  18.1 us
    reshape x1, local copies, waits for them, and re-layouts, per_device(): return (difference, received.reshape(1, devices, CAP, CUT * CUT))  1.96 us

commit v1 on v0

--- a/solution.py
+++ b/solution.py
@@ -90,12 +90,8 @@
             greet(a, d + 1)
 
     zero[...] = jnp.zeros_like(zero)
-    own = pltpu.make_async_copy(
-        t_ref, out_ref.at[pl.ds(EDGE, rows), pl.ds(LANE, cols)], lsem.at[0]
-    )
-    own.start()
-    blank_up = pltpu.make_async_copy(zero, out_ref.at[pl.ds(0, EDGE), :], lsem.at[1])
-    blank_down = pltpu.make_async_copy(zero, out_ref.at[pl.ds(EDGE + rows, EDGE), :], lsem.at[2])
+    blank_up = pltpu.make_async_copy(zero, out_ref.at[pl.ds(0, EDGE), :], lsem.at[0])
+    blank_down = pltpu.make_async_copy(zero, out_ref.at[pl.ds(EDGE + rows, EDGE), :], lsem.at[1])
 
     @pl.when(jnp.logical_not(has_up))
     def _():
@@ -165,7 +161,6 @@
     def _():
         blank_down.wait()
 
-    own.wait()
     copy(1, 2).wait()
     copy(1, 0).wait()
 
@@ -182,7 +177,7 @@
             pltpu.VMEM((EDGE, shape[1]), jnp.float32),
             pltpu.SemaphoreType.DMA((9,)),
             pltpu.SemaphoreType.DMA((9,)),
-            pltpu.SemaphoreType.DMA((3,)),
+            pltpu.SemaphoreType.DMA((2,)),
         ],
         compiler_params=pltpu.CompilerParams(collective_id=0, has_side_effects=True),
         name="halo",
@@ -190,12 +185,30 @@
 
 
 def tile_kernel(
-    off_ref, dest_ref, row_ref, col_ref, joined, science, across, down2, down,
-    diff_ref, out_ref,
-    window, r_hi, r_lo, images, gram, padded, mix, tally,
+    off_ref, dest_ref, row_ref, col_ref, template_in, edges_in, science_in, across_in, down2_in, down_in,
+    diff_out, out_ref,
+    joined, science, across, down2, down, diff_ref, sems, window, r_hi, r_lo, images, gram, padded, mix, tally,
 ):
     rows, cols = science.shape
     tall = rows + 2 * EDGE
+    fetches = []
+
+    def fetch(src, dst):
+        fetches.append(pltpu.make_async_copy(src, dst, sems.at[len(fetches)]))
+        fetches[-1].start()
+
+    middle = slice(EDGE, EDGE + rows)
+    fetch(template_in, joined.at[middle, LANE : LANE + cols])
+    fetch(edges_in.at[middle, LANE + cols :], joined.at[middle, LANE + cols :])
+    fetch(edges_in.at[middle, 0:LANE], joined.at[middle, 0:LANE])
+    fetch(edges_in.at[0:EDGE, :], joined.at[0:EDGE, :])
+    fetch(edges_in.at[EDGE + rows :, :], joined.at[EDGE + rows :, :])
+    fetch(across_in, across)
+    fetch(science_in, science)
+    fetch(down2_in, down2)
+    fetch(down_in, down)
+    for k in range(5):
+        fetches[k].wait()
     deep = r_hi.shape[1]
     sources = row_ref.shape[0]
     owners = out_ref.shape[0] // CAP
@@ -222,6 +235,8 @@
 
     r_hi[:, tall:, :] = jnp.zeros((9, deep - tall, cols), bf16)
     r_lo[:, tall:, :] = jnp.zeros((9, deep - tall, cols), bf16)
+
+    fetches[5].wait()
 
     @pl.loop(0, blocks)
     def _(b):
@@ -239,6 +254,8 @@
                 r_hi[3 * g + i, 0:tall, pl.ds(at, LANE)] = top
                 r_lo[3 * g + i, 0:tall, pl.ds(at, LANE)] = (part - top.astype(f32)).astype(bf16)
 
+    for k in range(6, 9):
+        fetches[k].wait()
     gram[...] = jnp.zeros_like(gram)
     images[18] = jnp.ones((STEP, cols), bf16)
     chunk = min(cols, 2 * LANE)
@@ -307,6 +324,7 @@
             mix[STEP : 2 * STEP, at : at + DEEP] = (total - hi.astype(f32)).astype(bf16)
     flat = weight(18)
 
+    stores = []
     for y0 in range(0, rows, STEP):
         size = min(STEP, rows - y0)
 
@@ -325,6 +343,12 @@
             for c in range(chunk // LANE):
                 padded[at // LANE + c, y0 : y0 + size, :] = value[:, c * LANE : (c + 1) * LANE]
 
+        span = slice(y0, y0 + size)
+        stores.append(
+            pltpu.make_async_copy(diff_ref.at[span], diff_out.at[span], sems.at[9 + len(stores)])
+        )
+        stores[-1].start()
+
     out_ref[...] = jnp.zeros_like(out_ref)
 
     @pl.loop(0, owners)
@@ -355,12 +379,16 @@
         stamp = jnp.where(lane2 < CUT, even, odd)
         out_ref[owner * CAP + slot] = stamp.astype(bf16)
 
-
-def tile(joined, science, offsets, dest, row, col, devices):
+    for store in stores:
+        store.wait()
+
+
+def tile(template, edges, science, offsets, dest, row, col, devices):
     rows, cols = science.shape
     across, down2, down = tables()
     smem = pl.BlockSpec(memory_space=pltpu.SMEM)
     vmem = pl.BlockSpec(memory_space=pltpu.VMEM)
+    hbm = pl.BlockSpec(memory_space=pl.ANY)
     deep = -(-rows // STEP) * STEP + DEEP - STEP
     bf16 = jnp.bfloat16
     return pl.pallas_call(
@@ -369,9 +397,16 @@
             jax.ShapeDtypeStruct((rows, cols), jnp.float32),
             jax.ShapeDtypeStruct((devices * CAP, CUT // 2, LANE), bf16),
         ),
-        in_specs=[smem] * 4 + [vmem] * 5,
-        out_specs=(vmem, vmem),
+        in_specs=[smem] * 4 + [hbm] * 6,
+        out_specs=(hbm, vmem),
         scratch_shapes=[
+            pltpu.VMEM(edges.shape, jnp.float32),
+            pltpu.VMEM((rows, cols), jnp.float32),
+            pltpu.VMEM(across.shape, bf16),
+            pltpu.VMEM(down2.shape, bf16),
+            pltpu.VMEM(down.shape, jnp.float32),
+            pltpu.VMEM((rows, cols), jnp.float32),
+            pltpu.SemaphoreType.DMA((9 + -(-rows // STEP),)),
             pltpu.VMEM((2, rows + 2 * EDGE, cols + LANE), bf16),
             pltpu.VMEM((9, deep, cols), bf16),
             pltpu.VMEM((9, deep, cols), bf16),
@@ -383,7 +418,7 @@
         ],
         compiler_params=pltpu.CompilerParams(vmem_limit_bytes=52 * 1024 * 1024),
         name="tile",
-    )(offsets, dest, row, col, joined, science, jnp.asarray(across), jnp.asarray(down2), jnp.asarray(down))
+    )(offsets, dest, row, col, template, edges, science, jnp.asarray(across), jnp.asarray(down2), jnp.asarray(down))
 
 
 def exchange_kernel(n_ra, n_dec, in_ref, out_ref, ssem, rsem, lsem):
@@ -449,9 +484,9 @@
     devices = n_ra * n_dec
 
     def per_device(template, science, offsets, source_dest, source_row, source_col):
-        joined = halo(template, n_ra, n_dec)
+        edges = halo(template, n_ra, n_dec)
         difference, outgoing = tile(
-            joined, science, offsets, source_dest, source_row, source_col, devices
+            template, edges, science, offsets, source_dest, source_row, source_col, devices
         )
         received = exchange(outgoing.reshape(devices, CAP, CUT // 2, LANE), n_ra, n_dec)
         return difference, received.reshape(1, devices, CAP, CUT * CUT)

time: 89.6 us -> 70.2 us (0.78)
  Pallas kernels: 84.5 us -> 64.4 us
    pallas_call x1, Pallas kernels: 33.1 us -> 14.6 us  [halo(): pl.pallas_call(functools.partial(halo_kernel, n_ra, n_dec), out_shape=jax...]
where the time goes in v1:
time: 70.2 us; the launch traced here: 69.4 us
  Pallas kernels  64.4 us (92%)
  local copies, waits for them, and re-layouts  3.5 us (5%)
  between operations  1.45 us (2%)
    pallas_call x1, Pallas kernels, tile(): pl.pallas_call(tile_kernel, out_shape=(jax.ShapeDtypeStruct((rows, cols),...  32.5 us
    pallas_call x1, Pallas kernels, exchange(): pl.pallas_call(functools.partial(exchange_kernel, n_ra, n_dec), out_shape...  17.4 us
    pallas_call x1, Pallas kernels, halo(): pl.pallas_call(functools.partial(halo_kernel, n_ra, n_dec), out_shape=jax...  14.6 us
    reshape x1, local copies, waits for them, and re-layouts, per_device(): return (difference, received.reshape(1, devices, CAP, CUT * CUT))  1.96 us
    unnamed x11, local copies, waits for them, and re-layouts  1.55 us

profile of v1, /device:TPU:15, one launch (start us, length us, event | category | flops | bytes accessed | tf_op | source)
XLA Modules:
  0.0 69.4 jit_solution(11922412878298493622)
XLA Ops:
  0.6 0.0 copy-start.1
  0.6 0.0 copy-start.2
  0.7 0.0 copy-start.4
  0.7 0.0 copy-start.3
  1.4 0.7 %copy.11.dest_ref = s32[32,1]{1,0:T(8,128)S(1)} copy(s32[32,1]{0,1:T(1,128)} %param.12) | data formatting | bytes 256 | tf_op args[3]
  2.1 14.6 %halo.1.edges_in = f32[288,1792]{1,0:T(8,128)} custom-call(f32[256,1024]{1,0:T(8,128)} %template_in.1), custom_call_target="tpu_custom_call" | custom-call | tf_op jit(solution)/shard_map/halo/pallas_call | solution.py:171
  16.7 0.0 copy-done.1
  16.7 0.0 copy-done.2
  16.7 0.0 copy-done.4
  16.7 0.0 copy-done.3
  16.7 32.5 %tile.1 = (f32[256,1024]{1,0:T(8,128)}, bf16[64,32,128]{2,1,0:T(8,128)(2,1)S(1)}) custom-call(s32[1,1]{1,0:T(1,128)S(6)} %copy.12.off_ref, s32[32,1]{1,0:T(8,128)S(1)} %copy.11.dest_ref, s32[32]{0:T(128)S(1)} %copy-done.3, s32[32]{0:T(128)S(1)} %copy-done.4, f32[256,1024]{1,0:T(8,128)} %template_in.1, f32[288,1792]{1,0:T(8,128)} %halo.1.edges_in, ...), custom_call_target="tpu_custom_call" | custom-call | tf_op jit(solution)/shard_map/tile/pallas_call | solution.py:394
  49.2 0.0 copy-start
  49.2 0.8 %copy-done = bf16[64,32,128]{2,1,0:T(8,128)(2,1)} copy-done((bf16[64,32,128]{2,1,0:T(8,128)(2,1)}, bf16[64,32,128]{2,1,0:T(8,128)(2,1)S(1)}, u32[]{:S(2)}) %copy-start) | copy-done | bytes 524312
  50.0 17.4 %exchange.1 = bf16[32,2,32,128]{3,2,1,0:T(8,128)(2,1)} custom-call(bf16[32,2,32,128]{3,2,1,0:T(8,128)(2,1)} %bitcast.3), custom_call_target="tpu_custom_call" | custom-call | tf_op jit(solution)/shard_map/exchange/pallas_call | solution.py:467
  67.4 2.0 %reshape.11 = bf16[1,32,2,4096]{3,2,1,0:T(2,128)(2,1)} reshape(bf16[32,2,32,128]{3,2,1,0:T(8,128)(2,1)} %exchange.1) | data formatting | bytes 1048576 | tf_op jit(solution)/shard_map/reshape | solution.py:492
Async XLA Ops:
  0.6 16.1 %copy-start.1 = (f32[9,96,128]{2,1,0:T(8,128)S(1)}, f32[9,96,128]{2,1,0:T(8,128)}, u32[]{:S(2)}) copy-start(f32[9,96,128]{2,1,0:T(8,128)} %constant.8.clone.down_in) | copy-start | bytes 1327108
  0.6 16.1 %copy-start.2 = (bf16[9,96,256]{2,1,0:T(8,128)(2,1)S(1)}, bf16[9,96,256]{2,1,0:T(8,128)(2,1)}, u32[]{:S(2)}) copy-start(bf16[9,96,256]{2,1,0:T(8,128)(2,1)} %constant.7.clone.down2_in) | copy-start | bytes 1327108
  0.7 16.1 %copy-start.4 = (s32[32]{0:T(128)S(1)}, s32[32]{0:T(128)}, u32[]{:S(2)}) copy-start(s32[32]{0:T(128)} %col_ref.1) | copy-start | bytes 388
  0.7 16.1 %copy-start.3 = (s32[32]{0:T(128)S(1)}, s32[32]{0:T(128)}, u32[]{:S(2)}) copy-start(s32[32]{0:T(128)} %row_ref.1) | copy-start | bytes 388
  49.2 0.8 %copy-start = (bf16[64,32,128]{2,1,0:T(8,128)(2,1)}, bf16[64,32,128]{2,1,0:T(8,128)(2,1)S(1)}, u32[]{:S(2)}) copy-start(bf16[64,32,128]{2,1,0:T(8,128)(2,1)S(1)} %get-tuple-element.5) | copy-start | bytes 1572868
